TPU v7x, 32 devices: a whole 2x2x4 slice. The times are simulated.
32 devices in a mesh: groups: 2 (over x), radius: 16 (over z, y, core).
Axes of the slice: x: 2, y: 2, z: 4, core: 2. Of those that a mesh axis runs over, the one named last changes fastest.
Arguments:
- states: float32 [8, 400, 2048], P('groups', None, 'radius'), parts along dimension 0, may hold values from -6 to 6
- dipole: float32 [400, 400], replicated, may hold values from -0.625 to 0.625
- pattern: int32 [25, 25], replicated, may hold values 0 or 1
- angular: int32 [400], replicated, may hold values from 0 to 11
- thresholds: float32 [400], replicated, may hold values from 0 to 2
- surface_profile: float32 [2, 2048], P(None, 'radius'), may hold values from 0.2 to 1.5
- pulse_field: float32 [4], P('groups'), parts along dimension 0, may hold values from -0.05 to 0.05
Outputs:
- final_states: float32 [8, 400, 2048], P('groups', None, 'radius'), parts along dimension 0
- gradient: float32 [4], P('groups'), parts along dimension 0
There are 2 independent parts, one for each index of `groups`. A program takes and returns all parts, laid end to end along the dimension named above; an argument that names none is the same for every part. Nothing has to cross between parts.
All inputs are finite; a program needn't handle non-finite values.
Results may differ from a plain program's by a relative error of at most 0.00019.
Values sent between devices are 32-bit elements; how exact they have to be, the bound alone decides.
A program may use at most 64 MiB of HBM per device.

v0:
```python
import math

import jax
import jax.numpy as jnp
from jax import lax
from jax.sharding import PartitionSpec as P

STEPS = 2
ORDER = 4


inner_radius = 20.0
spacing = 0.08
time_step = 0.005


def spread(value, axis, root):
    mine = lax.axis_index(axis) == root
    return lax.psum(jnp.where(mine, value, jnp.zeros_like(value)), axis)


def padded(cells, sides, width):
    for axis, dim in sides:
        count = lax.axis_size(axis)
        ends = count - 1
        head = lax.slice_in_dim(cells, 0, width, axis=dim)
        tail = lax.slice_in_dim(cells, cells.shape[dim] - width, cells.shape[dim], axis=dim)
        cells = jnp.concatenate(
            [
                lax.ppermute(tail, axis, [(i, (i + 1) % count) for i in range(ends)]),
                cells,
                lax.ppermute(head, axis, [((i + 1) % count, i) for i in range(ends)]),
            ],
            axis=dim,
        )
    return cells


def coupling_matrix(dipole, pattern, angular):
    channels = dipole.shape[0]
    blocks = pattern.shape[0]
    block_size = channels // blocks
    joined = jnp.maximum(pattern, pattern.T)
    block_owner = jnp.arange(channels, dtype=jnp.int32) // block_size
    block_pick = (block_owner[:, None] == jnp.arange(blocks, dtype=jnp.int32)[None, :]).astype(
        jnp.int32
    )
    block_mask = jnp.dot(jnp.dot(block_pick, joined), block_pick.T)
    selection = jnp.abs(angular[:, None] - angular[None, :]) == 1
    allowed = (block_mask > 0) & selection
    return jnp.where(allowed, 0.5 * (dipole + dipole.T), jnp.zeros_like(dipole))


def surface_pair(points):
    value_row = (
        4.0 * points[:, :, 0] - 6.0 * points[:, :, 1] + 4.0 * points[:, :, 2] - points[:, :, 3]
    )
    slope_row = (
        -13.0 / 3.0 * points[:, :, 0]
        + 9.5 * points[:, :, 1]
        - 7.0 * points[:, :, 2]
        + 11.0 / 6.0 * points[:, :, 3]
    )
    return jnp.stack([value_row, slope_row])


def apply_hamiltonian(
    extended,
    positions,
    profile_rows,
    boundary,
    coupling,
    thresholds,
    centrifugal,
    strength,
    power,
    grid_points,
):
    center = extended[:, :, 2:-2]
    radial_values = inner_radius + (positions + 1).astype(jnp.float32) * spacing
    kinetic = (
        -0.5
        / (spacing * spacing)
        * (
            -1.0 / 12.0 * (extended[:, :, :-4] + extended[:, :, 4:])
            + 4.0 / 3.0 * (extended[:, :, 1:-3] + extended[:, :, 3:-1])
            - 2.5 * center
        )
    )
    potential = (
        thresholds[:, None] + centrifugal[:, None] / (radial_values * radial_values)[None, :]
    ) * center
    mixed_rows = jnp.einsum("cd,kdr->kcr", coupling, center, precision=lax.Precision.HIGHEST)
    driven = (strength * radial_values)[None, None, :] * mixed_rows
    boundary_term = (
        boundary[0][:, :, None] * profile_rows[0][None, None, :]
        + boundary[1][:, :, None] * profile_rows[1][None, None, :]
    )
    hamiltonian = kinetic + potential + driven + boundary_term
    advanced = (
        time_step
        / power
        * jnp.stack([hamiltonian[1], -hamiltonian[0], hamiltonian[3], -hamiltonian[2]])
    )
    inside = (positions >= 0) & (positions < grid_points)
    return (jnp.where(inside[None, None, :], advanced, jnp.zeros_like(advanced)), mixed_rows)


def boundary_data(points):
    return spread(surface_pair(points), "radius", 0)


def per_device(states, dipole, pattern, angular, thresholds, surface_profile, pulse_field):
    local_rows = states.shape[2]
    devices = lax.axis_size("radius")
    grid_points = local_rows * devices
    first_point = lax.axis_index("radius") * local_rows
    coupling = coupling_matrix(dipole, pattern, angular)
    centrifugal = 0.5 * (angular * (angular + 1)).astype(jnp.float32)
    local_positions = first_point + jnp.arange(local_rows, dtype=jnp.int32)
    radial_values = inner_radius + (local_positions + 1).astype(jnp.float32) * spacing
    normalizer = math.sqrt(states.shape[1] * grid_points) * (inner_radius + grid_points * spacing)
    partials = []
    for step_index in range(STEPS):
        strength = pulse_field[step_index]
        summed = states
        taylor_term = states
        for power in range(1, ORDER + 1):
            boundary = boundary_data(taylor_term[:, :, :4])
            extended = padded(taylor_term, (("radius", 2),), 2)
            taylor_term, mixed_rows = apply_hamiltonian(
                extended,
                local_positions,
                surface_profile,
                boundary,
                coupling,
                thresholds,
                centrifugal,
                strength,
                power,
                grid_points,
            )
            if power == 1:
                mixed_state = mixed_rows
            summed = summed + taylor_term
        intersection = jnp.sum(
            radial_values[None, :] * (states[2] * mixed_state[1] - states[3] * mixed_state[0])
        )
        intersection = lax.psum(intersection, "radius")
        partials.append(intersection)
        states = summed
    gathered = jnp.stack(partials)
    return (states, gathered / normalizer)


def solution(mesh):
    return jax.shard_map(
        per_device,
        mesh=mesh,
        in_specs=(P("groups", None, "radius"), P(), P(), P(), P(), P(None, "radius"), P("groups")),
        out_specs=(P("groups", None, "radius"), P("groups")),
        check_vma=False,
    )
```

profile of v0, /device:TPU:1, one launch (start us, length us, event | category | flops | bytes accessed | tf_op | source)
XLA Modules:
  0.0 624.2 jit_solution(16780126876502364732)
XLA Ops:
  0.7 1.7 copy.1349
  2.4 4.5 collective-permute-start
  7.0 1.9 collective-permute-start.1
  10.2 56.0 %psum.70 = f32[2,4,400]{2,1,0:T(4,128)S(1)} all-reduce(f32[2,4,400]{2,1,0:T(4,128)S(1)} %maximum_select_fusion), channel_id=1, replica_groups=mesh['groups'=2,'radius'=16] {'radius'}, use_global_device_ids=true, to_apply=%region_0.1 | all-reduce | flops 3200 | bytes 25600 | tf_op jit(solution)/shard_map/psum | solution.py:19
  68.0 1.2 copy.1343
  69.3 2.6 fusion.2
  71.9 2.4 fusion.156
  74.3 1.7 copy.1344
  78.0 2.1 fusion.127
  80.1 1.2 broadcast_multiply_fusion
  81.3 1.8 copy.1366
  83.1 2.4 fusion.83
  87.6 2.7 fusion.123
  90.3 57.6 %psum.71 = f32[2,4,400]{2,1,0:T(4,128)S(1)} all-reduce(f32[2,4,400]{2,1,0:T(4,128)S(1)} %maximum_select_fusion.1), channel_id=1, replica_groups=mesh['groups'=2,'radius'=16] {'radius'}, use_global_device_ids=true, to_apply=%region_1.2 | all-reduce | flops 3200 | bytes 25600 | tf_op jit(solution)/shard_map/psum | solution.py:19
  147.9 3.6 collective-permute-start.2
  151.5 5.1 collective-permute-start.3
  156.6 2.5 copy.1351
  159.2 3.6 fusion.73
  164.8 2.7 fusion.121
  167.6 53.1 %psum.72 = f32[2,4,400]{2,1,0:T(4,128)S(1)} all-reduce(f32[2,4,400]{2,1,0:T(4,128)S(1)} %maximum_select_fusion.2), channel_id=1, replica_groups=mesh['groups'=2,'radius'=16] {'radius'}, use_global_device_ids=true, to_apply=%region_2.3 | all-reduce | flops 3200 | bytes 25600 | tf_op jit(solution)/shard_map/psum | solution.py:19
  220.6 3.6 collective-permute-start.4
  224.2 4.6 collective-permute-start.5
  228.9 2.6 copy.1353
  231.4 3.6 fusion.63
  237.1 2.7 fusion.119
  239.8 53.0 %psum.73 = f32[2,4,400]{2,1,0:T(4,128)S(1)} all-reduce(f32[2,4,400]{2,1,0:T(4,128)S(1)} %maximum_select_fusion.3), channel_id=1, replica_groups=mesh['groups'=2,'radius'=16] {'radius'}, use_global_device_ids=true, to_apply=%region_3.4 | all-reduce | flops 3200 | bytes 25600 | tf_op jit(solution)/shard_map/psum | solution.py:19
  292.9 3.6 collective-permute-start.6
  296.5 4.8 collective-permute-start.7
  301.3 2.5 copy.1355
  303.8 3.6 fusion.53
  309.0 5.1 fusion.105
  314.1 2.7 fusion.117
  316.9 2.5 copy.1357
  319.4 2.9 fusion.126
  322.3 1.8 copy.1367
  324.1 53.1 %psum.74 = f32[2,4,400]{2,1,0:T(4,128)S(1)} all-reduce(f32[2,4,400]{2,1,0:T(4,128)S(1)} %maximum_select_fusion.4), channel_id=1, replica_groups=mesh['groups'=2,'radius'=16] {'radius'}, use_global_device_ids=true, to_apply=%region_4.5 | all-reduce | flops 3200 | bytes 25600 | tf_op jit(solution)/shard_map/psum | solution.py:19
  377.1 3.6 collective-permute-start.8
  380.8 4.8 collective-permute-start.9
  385.6 1.8 fusion.129
  387.4 3.6 fusion.43
  391.8 1.2 fusion.106
  393.0 2.7 fusion.115
  395.8 53.1 %psum.75 = f32[2,4,400]{2,1,0:T(4,128)S(1)} all-reduce(f32[2,4,400]{2,1,0:T(4,128)S(1)} %maximum_select_fusion.5), channel_id=1, replica_groups=mesh['groups'=2,'radius'=16] {'radius'}, use_global_device_ids=true, to_apply=%region_5.6 | all-reduce | flops 3200 | bytes 25600 | tf_op jit(solution)/shard_map/psum | solution.py:19
  448.8 3.6 collective-permute-start.10
  452.4 4.6 collective-permute-start.11
  457.1 2.6 copy.1359
  459.6 3.6 fusion.33
  464.1 1.2 fusion.107
  465.3 2.7 fusion.113
  468.0 53.1 %psum.76 = f32[2,4,400]{2,1,0:T(4,128)S(1)} all-reduce(f32[2,4,400]{2,1,0:T(4,128)S(1)} %maximum_select_fusion.6), channel_id=1, replica_groups=mesh['groups'=2,'radius'=16] {'radius'}, use_global_device_ids=true, to_apply=%region_6.7 | all-reduce | flops 3200 | bytes 25600 | tf_op jit(solution)/shard_map/psum | solution.py:19
  521.1 3.6 collective-permute-start.12
  524.7 4.9 collective-permute-start.13
  529.6 2.5 copy.1361
  532.1 3.6 fusion.23
  536.5 1.2 fusion.108
  537.8 2.7 fusion.111
  540.5 53.0 %all-reduce = (f32[2,4,400]{2,1,0:T(4,128)S(1)}, f32[1]{0:T(128)}, f32[1]{0:T(128)}) all-reduce(f32[2,4,400]{2,1,0:T(4,128)S(1)} %maximum_select_fusion.7, f32[1]{0:T(128)} %bitcast.50, f32[1]{0:T(128)} %bitcast.48), channel_id=1, replica_groups=mesh['groups'=2,'radius'=16] {'radius'}, use_global_device_ids=true, to_apply=%region_7.8 | all-reduce | flops 3202 | bytes 25616 | tf_op jit(solution)/shard_map/psum | solution.py:19
  593.6 3.6 collective-permute-start.14
  597.2 4.6 collective-permute-start.15
  601.8 1.8 maximum_multiply_fusion.8
  603.6 2.6 copy.1363
  606.3 3.7 fusion.13
  611.6 10.9 %fusion.110 = f32[4,400,128]{1,0,2:T(4,128)S(1)} fusion(f32[1,400,128]{1,0,2:T(1,128)S(1)} %get-tuple-element.14, f32[1,400,128]{1,0,2:T(1,128)S(1)} %get-tuple-element.15, f32[1,400,128]{1,0,2:T(1,128)S(1)} %get-tuple-element.16, f32[1,400,128]{1,0,2:T(1,128)S(1)} %get-tuple-element.13, pred[128]{0:T(512)(128)(4,1)S(1)} %compare_and_fusion, ...), kind=kLoop, calls=%fused_computation.166 | loop fusion | flops 9830400 | bytes 8192128 | tf_op jit(solution)/shard_map/add | solution.py:145
  622.5 1.3 copy.1368
  (209 shorter events, 16.6 us)
Async XLA Ops:
  0.6 8.3 %copy-start = (f32[4,400,128]{2,1,0:T(8,128)S(1)}, f32[4,400,128]{2,1,0:T(8,128)}, u32[]{:S(2)}) copy-start(f32[4,400,128]{2,1,0:T(8,128)} %param.7) | copy-start | bytes 2457604
  0.6 65.6 %copy-start.66 = (f32[2]{0:T(128)S(1)}, f32[2]{0:T(128)}, u32[]{:S(2)}) copy-start(f32[2]{0:T(128)} %param.13) | copy-start | bytes 28
  0.6 67.3 %copy-start.62 = (s32[400]{0:T(512)S(1)}, s32[400]{0:T(512)}, u32[]{:S(2)}) copy-start(s32[400]{0:T(512)} %param.10) | copy-start | bytes 4804
  0.7 67.3 %copy-start.34 = (f32[400,400]{1,0:T(8,128)S(1)}, f32[400,400]{1,0:T(8,128)}, u32[]{:S(2)}) copy-start(f32[400,400]{1,0:T(8,128)} %param.8) | copy-start | bytes 1920004
  2.4 80.7 %collective-permute-start = (f32[4,400,2]{1,0,2:T(4,128)S(1)}, f32[4,400,2]{1,0,2:T(4,128)S(1)}, u32[]{:S(2)}, u32[]{:S(2)}) collective-permute-start(f32[4,400,2]{1,0,2:T(4,128)S(1)} %get-tuple-element.75), channel_id=1, source_target_pairs={{0,1},{1,2},{2,3},{3,4},{4,5},{5,6},{6,7},{7,8},{8,9},{9,10},{10,1... | collective-permute-start | bytes 38408 | tf_op jit(solution)/shard_map/ppermute | solution.py:30
  7.0 76.1 %collective-permute-start.1 = (f32[4,400,2]{1,0,2:T(4,128)S(1)}, f32[4,400,2]{1,0,2:T(4,128)S(1)}, u32[]{:S(2)}, u32[]{:S(2)}) collective-permute-start(f32[4,400,2]{1,0,2:T(4,128)S(1)} %get-tuple-element.76), channel_id=1, source_target_pairs={{1,0},{2,1},{3,2},{4,3},{5,4},{6,5},{7,6},{8,7},{9,8},{10,9},{11,1... | collective-permute-start | bytes 38408 | tf_op jit(solution)/shard_map/ppermute | solution.py:32
  9.7 59.5 %copy-start.61 = (s32[25,25]{1,0:T(8,128)S(1)}, s32[25,25]{1,0:T(8,128)}, u32[]{:S(2)}) copy-start(s32[25,25]{1,0:T(8,128)} %param.9) | copy-start | bytes 7504
  74.3 1.7 copy-start.67
  74.3 3.6 copy-start.64
  74.3 3.6 copy-start.65
  147.9 11.2 %collective-permute-start.2 = (f32[4,400,2]{1,0,2:T(4,128)S(1)}, f32[4,400,2]{1,0,2:T(4,128)S(1)}, u32[]{:S(2)}, u32[]{:S(2)}) collective-permute-start(f32[4,400,2]{1,0,2:T(4,128)S(1)} %get-tuple-element.67), channel_id=1, source_target_pairs={{0,1},{1,2},{2,3},{3,4},{4,5},{5,6},{6,7},{7,8},{8,9},{9,10},{10,1... | collective-permute-start | bytes 38408 | tf_op jit(solution)/shard_map/ppermute | solution.py:30
  151.5 7.6 %collective-permute-start.3 = (f32[4,400,2]{1,0,2:T(4,128)S(1)}, f32[4,400,2]{1,0,2:T(4,128)S(1)}, u32[]{:S(2)}, u32[]{:S(2)}) collective-permute-start(f32[4,400,2]{1,0,2:T(4,128)S(1)} %get-tuple-element.68), channel_id=1, source_target_pairs={{1,0},{2,1},{3,2},{4,3},{5,4},{6,5},{7,6},{8,7},{9,8},{10,9},{11,1... | collective-permute-start | bytes 38408 | tf_op jit(solution)/shard_map/ppermute | solution.py:32
  163.6 1.2 copy-start.10
  163.6 1.2 copy-start.13
  163.6 1.2 copy-start.16
  163.6 1.2 copy-start.19
  220.6 10.8 %collective-permute-start.4 = (f32[4,400,2]{1,0,2:T(4,128)S(1)}, f32[4,400,2]{1,0,2:T(4,128)S(1)}, u32[]{:S(2)}, u32[]{:S(2)}) collective-permute-start(f32[4,400,2]{1,0,2:T(4,128)S(1)} %get-tuple-element.59), channel_id=1, source_target_pairs={{0,1},{1,2},{2,3},{3,4},{4,5},{5,6},{6,7},{7,8},{8,9},{9,10},{10,1... | collective-permute-start | bytes 38408 | tf_op jit(solution)/shard_map/ppermute | solution.py:30
  224.2 7.2 %collective-permute-start.5 = (f32[4,400,2]{1,0,2:T(4,128)S(1)}, f32[4,400,2]{1,0,2:T(4,128)S(1)}, u32[]{:S(2)}, u32[]{:S(2)}) collective-permute-start(f32[4,400,2]{1,0,2:T(4,128)S(1)} %get-tuple-element.60), channel_id=1, source_target_pairs={{1,0},{2,1},{3,2},{4,3},{5,4},{6,5},{7,6},{8,7},{9,8},{10,9},{11,1... | collective-permute-start | bytes 38408 | tf_op jit(solution)/shard_map/ppermute | solution.py:32
  235.8 1.2 copy-start.22
  235.8 1.2 copy-start.25
  235.8 1.2 copy-start.28
  235.8 1.2 copy-start.31
  292.9 10.9 %collective-permute-start.6 = (f32[4,400,2]{1,0,2:T(4,128)S(1)}, f32[4,400,2]{1,0,2:T(4,128)S(1)}, u32[]{:S(2)}, u32[]{:S(2)}) collective-permute-start(f32[4,400,2]{1,0,2:T(4,128)S(1)} %get-tuple-element.51), channel_id=1, source_target_pairs={{0,1},{1,2},{2,3},{3,4},{4,5},{5,6},{6,7},{7,8},{8,9},{9,10},{10,1... | collective-permute-start | bytes 38408 | tf_op jit(solution)/shard_map/ppermute | solution.py:30
  296.5 7.3 %collective-permute-start.7 = (f32[4,400,2]{1,0,2:T(4,128)S(1)}, f32[4,400,2]{1,0,2:T(4,128)S(1)}, u32[]{:S(2)}, u32[]{:S(2)}) collective-permute-start(f32[4,400,2]{1,0,2:T(4,128)S(1)} %get-tuple-element.52), channel_id=1, source_target_pairs={{1,0},{2,1},{3,2},{4,3},{5,4},{6,5},{7,6},{8,7},{9,8},{10,9},{11,1... | collective-permute-start | bytes 38408 | tf_op jit(solution)/shard_map/ppermute | solution.py:32
  303.8 4.6 copy-start.26
  303.8 4.6 copy-start.29
  303.8 4.6 copy-start.32
  307.5 1.2 copy-start.14
  307.5 1.3 copy-start.17
  307.5 1.4 copy-start.20
  307.5 1.4 copy-start.23
  308.4 5.7 copy-start.35
  308.4 5.7 copy-start.37
  308.4 5.7 copy-start.39
  308.4 5.7 copy-start.41
  319.4 66.2 %copy-start.68 = (f32[128]{0:T(128)S(1)}, f32[128]{0:T(128)}, u32[]{:S(2)}) copy-start(f32[128]{0:T(128)} %multiply_add_fusion) | copy-start | bytes 1540
  319.4 67.9 %copy-start.63 = (f32[128]{0:T(128)S(1)}, f32[128]{0:T(128)}, u32[]{:S(2)}) copy-start(f32[128]{0:T(128)} %broadcast_multiply_fusion) | copy-start | bytes 1540
  377.1 10.2 %collective-permute-start.8 = (f32[4,400,2]{1,0,2:T(4,128)S(1)}, f32[4,400,2]{1,0,2:T(4,128)S(1)}, u32[]{:S(2)}, u32[]{:S(2)}) collective-permute-start(f32[4,400,2]{1,0,2:T(4,128)S(1)} %get-tuple-element.43), channel_id=1, source_target_pairs={{0,1},{1,2},{2,3},{3,4},{4,5},{5,6},{6,7},{7,8},{8,9},{9,10},{10,1... | collective-permute-start | bytes 38408 | tf_op jit(solution)/shard_map/ppermute | solution.py:30
  380.8 6.6 %collective-permute-start.9 = (f32[4,400,2]{1,0,2:T(4,128)S(1)}, f32[4,400,2]{1,0,2:T(4,128)S(1)}, u32[]{:S(2)}, u32[]{:S(2)}) collective-permute-start(f32[4,400,2]{1,0,2:T(4,128)S(1)} %get-tuple-element.44), channel_id=1, source_target_pairs={{1,0},{2,1},{3,2},{4,3},{5,4},{6,5},{7,6},{8,7},{9,8},{10,9},{11,1... | collective-permute-start | bytes 38408 | tf_op jit(solution)/shard_map/ppermute | solution.py:32
  391.8 1.2 copy-start.43
  391.8 1.2 copy-start.45
  448.8 10.8 %collective-permute-start.10 = (f32[4,400,2]{1,0,2:T(4,128)S(1)}, f32[4,400,2]{1,0,2:T(4,128)S(1)}, u32[]{:S(2)}, u32[]{:S(2)}) collective-permute-start(f32[4,400,2]{1,0,2:T(4,128)S(1)} %get-tuple-element.35), channel_id=1, source_target_pairs={{0,1},{1,2},{2,3},{3,4},{4,5},{5,6},{6,7},{7,8},{8,9},{9,10},{10,1... | collective-permute-start | bytes 38408 | tf_op jit(solution)/shard_map/ppermute | solution.py:30
  452.4 7.2 %collective-permute-start.11 = (f32[4,400,2]{1,0,2:T(4,128)S(1)}, f32[4,400,2]{1,0,2:T(4,128)S(1)}, u32[]{:S(2)}, u32[]{:S(2)}) collective-permute-start(f32[4,400,2]{1,0,2:T(4,128)S(1)} %get-tuple-element.36), channel_id=1, source_target_pairs={{1,0},{2,1},{3,2},{4,3},{5,4},{6,5},{7,6},{8,7},{9,8},{10,9},{11,1... | collective-permute-start | bytes 38408 | tf_op jit(solution)/shard_map/ppermute | solution.py:32
  521.1 11.0 %collective-permute-start.12 = (f32[4,400,2]{1,0,2:T(4,128)S(1)}, f32[4,400,2]{1,0,2:T(4,128)S(1)}, u32[]{:S(2)}, u32[]{:S(2)}) collective-permute-start(f32[4,400,2]{1,0,2:T(4,128)S(1)} %get-tuple-element.27), channel_id=1, source_target_pairs={{0,1},{1,2},{2,3},{3,4},{4,5},{5,6},{6,7},{7,8},{8,9},{9,10},{10,1... | collective-permute-start | bytes 38408 | tf_op jit(solution)/shard_map/ppermute | solution.py:30
  524.7 7.4 %collective-permute-start.13 = (f32[4,400,2]{1,0,2:T(4,128)S(1)}, f32[4,400,2]{1,0,2:T(4,128)S(1)}, u32[]{:S(2)}, u32[]{:S(2)}) collective-permute-start(f32[4,400,2]{1,0,2:T(4,128)S(1)} %get-tuple-element.28), channel_id=1, source_target_pairs={{1,0},{2,1},{3,2},{4,3},{5,4},{6,5},{7,6},{8,7},{9,8},{10,9},{11,1... | collective-permute-start | bytes 38408 | tf_op jit(solution)/shard_map/ppermute | solution.py:32
  593.6 12.6 %collective-permute-start.14 = (f32[4,400,2]{1,0,2:T(4,128)S(1)}, f32[4,400,2]{1,0,2:T(4,128)S(1)}, u32[]{:S(2)}, u32[]{:S(2)}) collective-permute-start(f32[4,400,2]{1,0,2:T(4,128)S(1)} %get-tuple-element.19), channel_id=1, source_target_pairs={{0,1},{1,2},{2,3},{3,4},{4,5},{5,6},{6,7},{7,8},{8,9},{9,10},{10,1... | collective-permute-start | bytes 38408 | tf_op jit(solution)/shard_map/ppermute | solution.py:30
  597.2 9.0 %collective-permute-start.15 = (f32[4,400,2]{1,0,2:T(4,128)S(1)}, f32[4,400,2]{1,0,2:T(4,128)S(1)}, u32[]{:S(2)}, u32[]{:S(2)}) collective-permute-start(f32[4,400,2]{1,0,2:T(4,128)S(1)} %get-tuple-element.20), channel_id=1, source_target_pairs={{1,0},{2,1},{3,2},{4,3},{5,4},{6,5},{7,6},{8,7},{9,8},{10,9},{11,1... | collective-permute-start | bytes 38408 | tf_op jit(solution)/shard_map/ppermute | solution.py:32
  606.2 4.8 copy-start.27
  606.2 4.8 copy-start.30
  606.2 4.8 copy-start.33
  606.2 4.8 copy-start.36
  606.2 4.8 copy-start.38
  606.2 4.8 copy-start.40
  606.2 4.8 copy-start.42
  606.2 4.8 copy-start.44
  606.3 4.8 copy-start.46
  606.3 4.8 copy-start.48
  606.3 4.8 copy-start.50
  606.3 4.8 copy-start.52
  606.3 4.8 copy-start.54
  610.1 1.2 copy-start.15
  610.1 1.3 copy-start.18
  610.1 1.4 copy-start.21
  610.1 1.4 copy-start.24
  (21 other events, 24.4 us)
where the time goes:
time: 633 us; the launch traced here: 624 us
  blocking collectives  432 us (68%)
  other arithmetic  68.8 us (11%)
  starting transfers between devices  65.1 us (10%)
  local copies, waits for them, and re-layouts  31.9 us (5%)
  matrix products  24 us (4%)
    psum x8, blocking collectives, spread(): return lax.psum(jnp.where(mine, value, jnp.zeros_like(value)), axis)  432 us
    ppermute x8, starting transfers between devices, padded(): lax.ppermute(head, axis, [((i + 1) % count, i) for i in range(ends)])  35.3 us
    ppermute x8, starting transfers between devices, padded(): lax.ppermute(tail, axis, [(i, (i + 1) % count) for i in range(ends)])  29.7 us
    add x8, other arithmetic, apply_hamiltonian(): hamiltonian = kinetic + potential + driven + boundary_term  27.6 us
    dot_general x8, matrix products, apply_hamiltonian(): jnp.einsum('cd,kdr->kcr', coupling, center, precision=lax.Precision.HIGHEST)  21.4 us
    dot_general x8, local copies, waits for them, and re-layouts, apply_hamiltonian(): jnp.einsum('cd,kdr->kcr', coupling, center, precision=lax.Precision.HIGHEST)  19.5 us
    add x2, other arithmetic, per_device(): summed = summed + taylor_term  16 us
  transfers between devices with their start and end apart: 16, of which 0 were waited for; matrix products, arithmetic and copies ran while one was open for 6% of the time, Pallas kernels for 0%

commit v1 on v0

v1 whole, which is shorter than its diff:
```python
import functools
import math

import jax
import jax.numpy as jnp
from jax import lax
from jax.experimental import pallas as pl
from jax.experimental.pallas import tpu as pltpu
from jax.sharding import PartitionSpec as P

STEPS = 2
ORDER = 4
inner_radius = 20.0
spacing = 0.08
time_step = 0.005

HALO = 2 * ORDER * STEPS
STRIP = HALO + 2
BASE = 20
ROWS = 16
CHUNKS = 3
TREE = (4, 2, 1)
MESH = pl.DeviceIdType.MESH
F32 = jnp.float32
BF16 = jnp.bfloat16


def coupling_matrix(dipole, pattern, angular):
    channels = dipole.shape[0]
    blocks = pattern.shape[0]
    block_size = channels // blocks
    joined = jnp.maximum(pattern, pattern.T)
    block_mask = jnp.repeat(jnp.repeat(joined, block_size, axis=0), block_size, axis=1)
    selection = jnp.abs(angular[:, None] - angular[None, :]) == 1
    allowed = (block_mask > 0) & selection
    return jnp.where(allowed, 0.5 * (dipole + dipole.T), jnp.zeros_like(dipole))


def halves(value):
    high = value.astype(BF16)
    return high, (value - high.astype(F32)).astype(BF16)


def kernel(
    count, channels, states, lhs, chan, prof, pulse, out, grad,
    to_left, to_right, from_left, from_right, strip,
    term, total, rhs, mixed, edge, surface, pot, partial, gathered,
    halo_send, halo_recv, strip_send, strip_recv, grad_send, grad_recv,
):
    me = lax.axis_index("radius")
    size = 128
    has_left, has_right = me > 0, me < count - 1
    lane = lax.broadcasted_iota(jnp.int32, (1, size), 1)

    barrier = pltpu.get_barrier_semaphore()

    def greet(d, _):
        other = lax.rem(me + d, count)
        pl.semaphore_signal(barrier, inc=1, device_id={"radius": other}, device_id_type=MESH)
        return 0

    lax.fori_loop(1, count, greet, 0)

    low = lane < 64
    low_quarter = lax.rem(lane, 64) < 32
    padded_prof = jnp.concatenate([prof[...], jnp.zeros((6, size), F32)], axis=0)
    turned_prof = pltpu.roll(padded_prof, 64, 1)

    def pack(start, rows, parts):
        a, b, c, d = parts
        left = jnp.where(low_quarter, jnp.where(low, a, b), pltpu.roll(jnp.where(low, c, d), 32, 1))
        right = jnp.where(low_quarter, pltpu.roll(jnp.where(low, d, c), 96, 1), jnp.where(low, b, a))
        to_left[start : start + rows, :] = left
        to_right[start : start + rows, :] = right

    for start in range(0, channels, ROWS):
        rows = slice(start, start + ROWS)
        a, c = states[0, rows, :], states[2, rows, :]
        b, d = pltpu.roll(states[1, rows, :], 64, 1), pltpu.roll(states[3, rows, :], 64, 1)
        pack(start, ROWS, (a, b, c, d))
        for pair, (first, second) in enumerate(((a, b), (c, d))):
            term[pair, rows, 0:size] = first
            term[pair, rows, size : 2 * size] = second
    pack(channels, 8, (padded_prof, turned_prof, padded_prof, turned_prof))

    @pl.when(me == 0)
    def _():
        strip[...] = to_left[...]

    pl.semaphore_wait(barrier, count - 1)

    def halo_copy(source, target, which, other):
        return pltpu.make_async_remote_copy(
            src_ref=source, dst_ref=target, send_sem=halo_send.at[which],
            recv_sem=halo_recv.at[which], device_id={"radius": other}, device_id_type=MESH,
        )

    left_copy = halo_copy(to_left, from_right, 0, jnp.maximum(me - 1, 0))
    right_copy = halo_copy(to_right, from_left, 1, jnp.minimum(me + 1, count - 1))

    chunk = (channels + 8) // CHUNKS
    children = []
    for step in TREE:
        child = me + step
        mine = (lax.rem(me, 2 * step) == 0) if step < TREE[0] else (lax.rem(me, step) == 0)
        children.append((child, mine & (child < count)))

    def strip_copy(part, which):
        rows = pl.ds(part * chunk, chunk)
        return pltpu.make_async_remote_copy(
            src_ref=strip.at[rows, :], dst_ref=strip.at[rows, :],
            send_sem=strip_send.at[which, part], recv_sem=strip_recv.at[part],
            device_id={"radius": jnp.minimum(children[which][0], count - 1)}, device_id_type=MESH,
        )

    def send_on(part):
        for which in range(len(TREE)):
            @pl.when(children[which][1])
            def _():
                strip_copy(part, which).start()

    @pl.when(me == 0)
    def _():
        for part in range(CHUNKS):
            send_on(part)

    @pl.when(has_left)
    def _():
        left_copy.start()

    @pl.when(has_right)
    def _():
        right_copy.start()

    @pl.when(me > 0)
    def _():
        for part in range(CHUNKS):
            strip_copy(part, 0).wait_recv()
            send_on(part)

    second = (lane >= 48) & (lane < 112)
    place = jnp.where(second, lax.rem(lane + 64, size), lane)
    in_right, in_left = place < HALO, place >= size - HALO
    in_strip = (place >= BASE) & (place < BASE + STRIP)
    here = me * size
    extra = jnp.where(in_right, here + size + place, jnp.where(in_left, here - size + place, place - BASE))
    valid = (in_right & has_right) | (in_left & has_left) | in_strip
    extra = jnp.where(valid, extra, 0)
    keep = jnp.where(valid, 1.0, 0.0).astype(F32)
    flip = jnp.where(second, -keep, keep)
    positions = jnp.concatenate([here + lane, here + lax.rem(lane + 64, size), extra], axis=1)
    radial = inner_radius + (positions + 1).astype(F32) * spacing
    inverse = 1.0 / (radial * radial)

    @pl.when(has_right)
    def _():
        left_copy_in = halo_copy(to_left, from_right, 0, jnp.minimum(me + 1, count - 1))
        left_copy_in.wait_recv()

    @pl.when(jnp.logical_not(has_right))
    def _():
        from_right[...] = jnp.zeros_like(from_right)

    @pl.when(has_left)
    def _():
        right_copy_in = halo_copy(to_right, from_left, 1, jnp.maximum(me - 1, 0))
        right_copy_in.wait_recv()

    @pl.when(jnp.logical_not(has_left))
    def _():
        from_left[...] = jnp.zeros_like(from_left)

    def unpack(start, rows, pair):
        cut = slice(start, start + rows)
        right, left, inner = from_right[cut, :], from_left[cut, :], strip[cut, :]
        if pair == 1:
            right, left = pltpu.roll(right, 96, 1), pltpu.roll(left, 32, 1)
        inner = pltpu.roll(inner, BASE if pair == 0 else BASE + 96, 1)
        gathered_lanes = jnp.where(in_right, right, jnp.where(in_left, left, inner))
        return jnp.where(valid, gathered_lanes, 0.0)

    def shift(value, amount):
        return pltpu.roll(value, amount % size, 1)

    near = (lax.rem(lane, 64) >= BASE) & (lax.rem(lane, 64) < BASE + 4)

    def store_split(pair, start, tiles):
        for tile, value in enumerate(tiles):
            cols = slice(tile * size, (tile + 1) * size)
            high, rest = halves(value)
            rhs[pair, start : start + ROWS, cols] = high
            rhs[pair, channels + start : channels + start + ROWS, cols] = rest
            rhs[pair, 2 * channels + start : 2 * channels + start + ROWS, cols] = high
        points = jnp.where(near, tiles[2], 0.0)
        high = points.astype(BF16).astype(F32)
        rest = points - high
        edge[pair, start : start + ROWS, :] = (high + shift(rest, 8) + shift(high, 16)).astype(BF16)

    prof_extra = unpack(channels, 8, 0)
    prof_all = jnp.concatenate([padded_prof, turned_prof, prof_extra], axis=1)
    row = lax.broadcasted_iota(jnp.int32, (size, 1), 0)
    offset = lax.rem(row, 64) - BASE
    point = lax.rem(offset + 64, 8)
    used = (offset >= 0) & (offset < 24) & (point < 4)

    def weights(values):
        found = jnp.zeros((size, 1), F32)
        for index, value in enumerate(values):
            found = jnp.where(used & (point == index), value, found)
        return found

    value_weight = weights((4.0, -6.0, 4.0, -1.0))
    slope_weight = weights((-13.0 / 3.0, 9.5, -7.0, 11.0 / 6.0))
    owner = jnp.concatenate([jnp.zeros((1, size), jnp.int32), jnp.ones((1, size), jnp.int32), second.astype(jnp.int32)], axis=1)
    full = value_weight * prof_all[0:1, :] + slope_weight * prof_all[1:2, :]
    full = jnp.where((row // 64) == owner, full, 0.0)
    high = full.astype(BF16).astype(F32)
    surface[...] = jnp.where(offset < 16, high, full - high).astype(BF16)

    rhs[:, 3 * channels :, :] = jnp.zeros((2, rhs.shape[1] - 3 * channels, 3 * size), BF16)
    diagonal = 1.25 / (spacing * spacing)
    for start in range(0, channels, ROWS):
        rows = slice(start, start + ROWS)
        pot[rows, :] = chan[rows, 0:1] + chan[rows, 1:2] * inverse + diagonal
        for pair in range(2):
            tiles = [term[pair, rows, 0:size], term[pair, rows, size : 2 * size], unpack(start, ROWS, pair)]
            term[pair, rows, 2 * size :] = tiles[2]
            store_split(pair, start, tiles)
            total[0, pair, rows, :] = jnp.concatenate(tiles, axis=1)
            total[1, pair, rows, :] = jnp.zeros((ROWS, 3 * size), F32)

    far_weight = 0.5 / (spacing * spacing) / 12.0
    near_weight = -0.5 / (spacing * spacing) * 4.0 / 3.0

    def stencil(first, other, extra_tile):
        results = [None] * 3
        for distance, weight in ((1, near_weight), (2, far_weight)):
            for amount in (distance, -distance):
                ra, rb, rx = shift(first, amount), shift(other, amount), shift(extra_tile, amount)
                if amount > 0:
                    seam = lane < amount
                    middle = (lane >= 64) & (lane < 64 + amount)
                else:
                    seam = lane >= size + amount
                    middle = (lane >= 64 + amount) & (lane < 64)
                moved = (
                    jnp.where(seam, rx, ra),
                    jnp.where(middle, rx, rb),
                    jnp.where(seam, ra, jnp.where(middle, rb, rx)),
                )
                if amount > 0:
                    ahead = moved
            for tile in range(3):
                both = weight * (ahead[tile] + moved[tile])
                results[tile] = both if results[tile] is None else results[tile] + both
        return results

    def grad_copy(other, slot):
        return pltpu.make_async_remote_copy(
            src_ref=partial, dst_ref=gathered.at[slot], send_sem=grad_send.at[other],
            recv_sem=grad_recv.at[slot], device_id={"radius": other}, device_id_type=MESH,
        )

    def one_step(step, _):
        strength = pulse[step]
        driven = strength * radial

        def one_term(index, _):
            power = index + 1
            scale = time_step / power.astype(F32)
            odd = lax.rem(power, 2)
            signed = jnp.where(odd == 1, -scale, scale)
            for pair in range(2):
                mixed[pair] = jnp.dot(lhs[...], rhs[pair], preferred_element_type=F32)

            @pl.when(index == 0)
            def _():
                found = jnp.zeros((8, size), F32)
                for start in range(0, channels, ROWS):
                    rows = slice(start, start + ROWS)
                    turned = shift(mixed[0, rows, size : 2 * size], 64) * term[1, rows, 0:size]
                    straight = shift(term[1, rows, size : 2 * size], 64) * mixed[0, rows, 0:size]
                    both = turned - straight
                    found = found + both[0:8] + both[8:16]
                partial[step] = found * radial[:, 0:size]

                @pl.when(step == STEPS - 1)
                def _():
                    def send(d, _):
                        grad_copy(lax.rem(me + d, count), me).start()
                        return 0

                    lax.fori_loop(1, count, send, 0)

            for pair in range(2):
                bound = jnp.dot(edge[pair], surface[...], preferred_element_type=F32)
                for start in range(0, channels, ROWS):
                    rows = slice(start, start + ROWS)
                    now = [term[pair, rows, t * size : (t + 1) * size] for t in range(3)]
                    moved = stencil(*now)
                    new = []
                    for tile in range(3):
                        cols = slice(tile * size, (tile + 1) * size)
                        value = moved[tile] + pot[rows, cols] * now[tile]
                        value = value + driven[:, cols] * mixed[pair, rows, cols] + bound[rows, cols]
                        factor = (signed, -signed, signed * flip)[tile]
                        value = factor * value
                        new.append(value)
                        term[pair, rows, cols] = value
                        total[odd, pair, rows, cols] += value
                    store_split(pair, start, new)
            return 0

        lax.fori_loop(0, ORDER, one_term, 0)

        for pair in range(2):
            for start in range(0, channels, ROWS):
                rows = slice(start, start + ROWS)
                tiles = []
                for tile in range(3):
                    cols = slice(tile * size, (tile + 1) * size)
                    source = (1, 0, 2)[tile]
                    turned = shift(total[1, pair, rows, source * size : (source + 1) * size], 64)
                    tiles.append(total[0, pair, rows, cols] + turned)
                for tile in range(3):
                    cols = slice(tile * size, (tile + 1) * size)
                    term[pair, rows, cols] = tiles[tile]
                    total[0, pair, rows, cols] = tiles[tile]
                    total[1, pair, rows, cols] = jnp.zeros((ROWS, size), F32)
                store_split(pair, start, tiles)
        return 0

    lax.fori_loop(0, STEPS, one_step, 0)

    for pair in range(2):
        for start in range(0, channels, ROWS):
            rows = slice(start, start + ROWS)
            out[2 * pair, rows, :] = term[pair, rows, 0:size]
            out[2 * pair + 1, rows, :] = shift(term[pair, rows, size : 2 * size], 64)

    gathered[me] = partial[...]

    def collect(d, _):
        other = lax.rem(me + d, count)
        copy = grad_copy(other, other)
        copy.wait_recv()
        return 0

    lax.fori_loop(1, count, collect, 0)
    normalizer = math.sqrt(channels * count * size) * (inner_radius + count * size * spacing)
    for step in range(STEPS):
        found = jnp.zeros((8, size), F32)
        for index in range(count):
            found = found + gathered[index, step]
        grad[step] = jnp.sum(found) / normalizer

    def finish(d, _):
        grad_copy(lax.rem(me + d, count), me).wait_send()
        return 0

    lax.fori_loop(1, count, finish, 0)

    @pl.when(has_left)
    def _():
        left_copy.wait_send()

    @pl.when(has_right)
    def _():
        right_copy.wait_send()

    for which in range(len(TREE)):
        @pl.when(children[which][1])
        def _():
            for part in range(CHUNKS):
                strip_copy(part, which).wait_send()


def per_device(count, states, dipole, pattern, angular, thresholds, surface_profile, pulse_field):
    channels = states.shape[1]
    size = states.shape[2]
    coupling = coupling_matrix(dipole, pattern, angular)
    rounded = lax.reduce_precision(coupling, 8, 7)
    high, rest = rounded.astype(BF16), (coupling - rounded).astype(BF16)
    depth = -(-3 * channels // 256) * 256
    lhs = jnp.concatenate([high, high, rest, jnp.zeros((channels, depth - 3 * channels), BF16)], axis=1)
    centrifugal = 0.5 * (angular * (angular + 1)).astype(F32)
    chan = jnp.stack([thresholds, centrifugal], axis=1)
    vmem = pl.BlockSpec(memory_space=pltpu.VMEM)
    smem = pl.BlockSpec(memory_space=pltpu.SMEM)
    message = pltpu.VMEM((channels + 8, size), F32)
    wide = (2, channels, 3 * size)
    return pl.pallas_call(
        functools.partial(kernel, count, channels),
        out_shape=(
            jax.ShapeDtypeStruct(states.shape, F32),
            jax.ShapeDtypeStruct(pulse_field.shape, F32),
        ),
        in_specs=[vmem, vmem, vmem, vmem, smem],
        out_specs=(vmem, smem),
        scratch_shapes=[
            message, message, message, message, message,
            pltpu.VMEM(wide, F32),
            pltpu.VMEM((2,) + wide, F32),
            pltpu.VMEM((2, depth, 3 * size), BF16),
            pltpu.VMEM(wide, F32),
            pltpu.VMEM((2, channels, size), BF16),
            pltpu.VMEM((size, 3 * size), BF16),
            pltpu.VMEM((channels, 3 * size), F32),
            pltpu.VMEM((STEPS, 8, size), F32),
            pltpu.VMEM((count, STEPS, 8, size), F32),
            pltpu.SemaphoreType.DMA((2,)),
            pltpu.SemaphoreType.DMA((2,)),
            pltpu.SemaphoreType.DMA((len(TREE), CHUNKS)),
            pltpu.SemaphoreType.DMA((CHUNKS,)),
            pltpu.SemaphoreType.DMA((count,)),
            pltpu.SemaphoreType.DMA((count,)),
        ],
        compiler_params=pltpu.CompilerParams(
            collective_id=0, has_side_effects=True, vmem_limit_bytes=48 * 1024 * 1024
        ),
        cost_estimate=pl.CostEstimate(flops=8000000000, bytes_accessed=4000000, transcendentals=0),
    )(states, lhs, chan, surface_profile, pulse_field)


def solution(mesh):
    return jax.shard_map(
        functools.partial(per_device, mesh.shape["radius"]),
        mesh=mesh,
        in_specs=(P("groups", None, "radius"), P(), P(), P(), P(), P(None, "radius"), P("groups")),
        out_specs=(P("groups", None, "radius"), P("groups")),
        check_vma=False,
    )
```

time: 633 us -> 89.4 us (0.14)
  the two profiles are of different devices: /device:TPU:1 before, /device:TPU:29 now
where the time goes in v1:
time: 89.4 us; the launch traced here: 89.2 us
  Pallas kernels  81.2 us (91%)
  local copies, waits for them, and re-layouts  6.75 us (8%)
    pallas_call x1, Pallas kernels, per_device(): pl.pallas_call(functools.partial(kernel, count, channels), out_shape=(jax...  81.2 us
    unnamed x18, local copies, waits for them, and re-layouts  4.6 us

profile of v1, /device:TPU:29, one launch (start us, length us, event | category | flops | bytes accessed | tf_op | source)
XLA Modules:
  0.0 89.2 jit_solution(1422859612416784423)
XLA Ops:
  0.6 0.0 copy-start.4
  0.6 1.4 %copy.26 = f32[400,400]{0,1:T(8,128)S(1)} copy(f32[400,400]{1,0:T(8,128)} %param.8) | data formatting | bytes 1280000 | tf_op args[1]
  2.1 0.0 copy-done.4
  2.1 0.0 copy-start.3
  2.1 0.1 copy.23
  2.2 0.1 copy.24
  2.4 0.1 broadcast_in_dim.15
  2.4 0.0 copy-start.5
  2.4 0.4 copy.25
  2.8 0.4 copy-done.3
  3.2 0.0 copy-done.5
  3.2 0.5 fusion
  3.7 0.0 copy-start
  3.7 1.4 %concatenate.3.lhs = bf16[400,1280]{1,0:T(8,128)(2,1)S(1)} concatenate(bf16[400,400]{1,0:T(8,128)(2,1)S(1)} %get-tuple-element.3, bf16[400,400]{1,0:T(8,128)(2,1)S(1)} %get-tuple-element.3, bf16[400,400]{1,0:T(8,128)(2,1)S(1)} %get-tuple-element.2, bf16[400,80]{1,0:T(8,128)(2,1)S(1)} %broadcast_in_dim.17), dimensions={1} | concatenate | bytes 2048000 | tf_op jit(solution)/shard_map/concatenate | solution.py:385
  5.2 0.0 copy-start.6
  5.2 0.7 copy-done.6
  5.9 0.0 copy-start.1
  5.9 0.0 copy-start.2
  5.9 0.1 copy.27.chan
  6.1 0.0 copy-done
  6.1 0.5 copy-done.1
  6.6 0.0 copy-done.2
  6.6 81.2 %shard_map.86 = (f32[4,400,128]{2,1,0:T(8,128)S(1)}, f32[2]{0:T(128)S(1)}) custom-call(f32[4,400,128]{2,1,0:T(8,128)S(1)} %copy-done, bf16[400,1280]{1,0:T(8,128)(2,1)S(1)} %concatenate.3.lhs, f32[400,2]{1,0:T(8,128)S(1)} %copy.27.chan, f32[2,128]{1,0:T(2,128)S(1)} %copy-done.1, f32[2]{0:T(128)S(1)} %copy-done.2), custom_call_target="tpu_custom_call" | custom-call | flops 8000000000 | bytes 4000000 | tf_op jit(solution)/shard_map/pallas_call | solution.py:392
  87.8 0.9 %copy.30 = f32[4,400,128]{2,1,0:T(8,128)} copy(f32[4,400,128]{2,1,0:T(8,128)S(1)} %get-tuple-element.6) | data formatting | bytes 1638400
  88.7 0.5 copy.31
  (5 shorter events, 0.1 us)
Async XLA Ops:
  0.6 1.5 %copy-start.4 = (s32[25,25]{1,0:T(8,128)S(1)}, s32[25,25]{1,0:T(8,128)}, u32[]{:S(2)}) copy-start(s32[25,25]{1,0:T(8,128)} %param.9) | copy-start | bytes 7504
  2.1 1.2 %copy-start.3 = (f32[400,400]{1,0:T(8,128)S(1)}, f32[400,400]{1,0:T(8,128)}, u32[]{:S(2)}) copy-start(f32[400,400]{1,0:T(8,128)} %param.8) | copy-start | bytes 1920004
  2.4 0.8 copy-start.5
  3.7 2.3 %copy-start = (f32[4,400,128]{2,1,0:T(8,128)S(1)}, f32[4,400,128]{2,1,0:T(8,128)}, u32[]{:S(2)}) copy-start(f32[4,400,128]{2,1,0:T(8,128)} %states.1) | copy-start | bytes 2457604
  5.2 0.7 copy-start.6
  5.9 0.7 copy-start.1
  5.9 0.7 copy-start.2
